TPU v7x, 32 devices: a whole 2x2x4 slice. The times are simulated.
32 devices in a mesh: groups: 2 (over y), vocab: 4 (over z), rows: 4 (over x, core).
Axes of the slice: x: 2, y: 2, z: 4, core: 2. Of those that a mesh axis runs over, the one named last changes fastest.
Arguments:
- student_hidden: bfloat16 [3584, 3072], P('vocab', ('groups', 'rows')), parts along dimension 1, may hold values from -180 to 180
- teacher_hidden: bfloat16 [5120, 3072], P('vocab', ('groups', 'rows')), parts along dimension 1, may hold values from -180 to 180
- teacher_head: bfloat16 [3, 5120, 512], P(None, None, 'vocab'), may hold values from -0.3125 to 0.3125
- student_head: bfloat16 [3584, 512], P(None, 'vocab'), may hold values from -0.3125 to 0.3125
- teacher_pick: int32 [3072], P(('groups', 'rows')), parts along dimension 0, may hold values from 0 to 2
- owner: int32 [8, 4], P('groups'), parts along dimension 0, may hold values from 0 to 3, as said below
Outputs:
- forward_kl: float32 [3072], P(('groups', 'rows')), parts along dimension 0
- reverse_kl: float32 [3072], P(('groups', 'rows')), parts along dimension 0
- grad_hidden: bfloat16 [3584, 3072], P('vocab', ('groups', 'rows')), parts along dimension 1
There are 2 independent parts, one for each index of `groups`. A program takes and returns all parts, laid end to end along the dimension named above; an argument that names none is the same for every part. Nothing has to cross between parts.
Inputs may be any that keep to these rules, and one draw needn't show every extreme that they name: In each round, owner is a permutation of the row blocks; the 4 entries of each column are distinct, so no row block sends two sub-blocks to the same owner.
All inputs are finite; a program needn't handle non-finite values.
Results may differ from a plain program's by a relative error of at most 0.005.
Values may be sent and summed in bfloat16 or wider, within the bound.
A program may use at most 64 MiB of HBM per device.

v0:
```python
import jax
import jax.numpy as jnp
from jax import lax
from jax.sharding import PartitionSpec as P


def local(student_hidden, teacher_hidden, teacher_head, student_head, teacher_pick, owner):
    rows_local = student_hidden.shape[1]
    round_count = owner.shape[0]
    sub_rows = rows_local // round_count
    row_devices = lax.axis_size("rows")
    own_rank = lax.axis_index("rows")
    all_ranks = jnp.arange(row_devices, dtype=jnp.int32)
    routed_parts = []
    for round_id in range(round_count):
        row_block = teacher_hidden[:, round_id * sub_rows : (round_id + 1) * sub_rows]
        gathered = lax.all_gather(row_block, "rows", axis=1, tiled=True)
        source = jnp.sum(jnp.where(owner[round_id] == own_rank, all_ranks, 0))
        routed_parts.append(lax.dynamic_slice_in_dim(gathered, source * sub_rows, sub_rows, 1))
    routed = jnp.concatenate(routed_parts, axis=1)
    teacher_count = teacher_head.shape[0]
    row_order = jnp.argsort(teacher_pick, stable=True)
    back_order = jnp.argsort(row_order, stable=True)
    group_sizes = jnp.sum(
        (teacher_pick[None, :] == jnp.arange(teacher_count, dtype=jnp.int32)[:, None]).astype(
            jnp.int32
        ),
        axis=1,
    )
    routed_sorted = routed[:, row_order]
    voc_local = student_head.shape[1]
    empty_logits = jnp.zeros((rows_local, voc_local), jnp.float32)
    head_rows = teacher_head
    sorted_logits = empty_logits + lax.ragged_dot(
        lax.all_gather(routed_sorted, "vocab", axis=0, tiled=True).T,
        head_rows,
        group_sizes,
        preferred_element_type=jnp.float32,
    )
    teacher_logits = sorted_logits[back_order]
    head_rows = student_head
    student_logits = lax.dot_general(
        lax.all_gather(student_hidden, "vocab", axis=0, tiled=True),
        head_rows,
        (((0,), (0,)), ((), ())),
        preferred_element_type=jnp.float32,
    )
    t_peak, s_peak = lax.pmax(
        (jnp.max(teacher_logits, axis=1), jnp.max(student_logits, axis=1)), "vocab"
    )
    t_total, s_total = lax.psum(
        (
            jnp.sum(jnp.exp(teacher_logits - t_peak[:, None]), axis=1),
            jnp.sum(jnp.exp(student_logits - s_peak[:, None]), axis=1),
        ),
        "vocab",
    )
    log_teacher = teacher_logits - (t_peak + jnp.log(t_total))[:, None]
    log_student = student_logits - (s_peak + jnp.log(s_total))[:, None]
    p_teacher = jnp.exp(log_teacher)
    p_student = jnp.exp(log_student)
    forward_kl, reverse_kl = lax.psum(
        (
            jnp.sum(p_teacher * (log_teacher - log_student), axis=1),
            jnp.sum(p_student * (log_student - log_teacher), axis=1),
        ),
        "vocab",
    )
    logit_grad = (
        p_student - p_teacher + p_student * (log_student - log_teacher - reverse_kl[:, None])
    ).astype(jnp.bfloat16)
    out_rows = student_head.shape[0] // lax.axis_size("vocab")
    head_rows = student_head
    grad_all = lax.psum(
        lax.dot_general(
            head_rows, logit_grad, (((1,), (1,)), ((), ())), preferred_element_type=jnp.float32
        ),
        "vocab",
    )
    grad_hidden = lax.dynamic_slice_in_dim(
        grad_all, lax.axis_index("vocab") * out_rows, out_rows, 0
    )
    return (forward_kl, reverse_kl, grad_hidden.astype(jnp.bfloat16))


def solution(mesh):
    placed = (
        P("vocab", ("groups", "rows")),
        P("vocab", ("groups", "rows")),
        P(None, None, "vocab"),
        P(None, "vocab"),
        P(("groups", "rows")),
        P("groups", None),
    )
    return jax.shard_map(
        local,
        mesh=mesh,
        in_specs=placed,
        out_specs=(P(("groups", "rows")), P(("groups", "rows")), P("vocab", ("groups", "rows"))),
        check_vma=False,
    )
```

profile of v0, /device:TPU:0, one launch (start us, length us, event | category | flops | bytes accessed | tf_op | source)
XLA Modules:
  0.0 381.6 jit_solution(2853217677515965472)
XLA Ops:
  7.2 0.7 all-gather.4.cloned.1.call-update
  8.0 1.6 fusion.3
  12.2 1.9 fusion.7
  14.1 0.2 copy.21
  14.3 0.2 copy.23
  14.4 0.2 copy.22
  14.6 0.2 copy.24
  14.8 3.8 sort.31
  18.6 11.1 %all_gather.21 = bf16[1280,384]{0,1:T(8,128)(2,1)S(1)} all-gather(bf16[1280,96]{0,1:T(8,128)(2,1)S(1)} %copy.24), channel_id=1, replica_groups=mesh['groups'=2,'vocab'=4,'rows'=4] {'rows'}, dimensions={1}, use_global_device_ids=true | all-gather | bytes 1228800 | tf_op jit(solution)/shard_map/all_gather | solution.py:17
  29.8 9.8 %all_gather.19 = bf16[1280,384]{0,1:T(8,128)(2,1)S(1)} all-gather(bf16[1280,96]{0,1:T(8,128)(2,1)S(1)} %copy.22), channel_id=1, replica_groups=mesh['groups'=2,'vocab'=4,'rows'=4] {'rows'}, dimensions={1}, use_global_device_ids=true | all-gather | bytes 1228800 | tf_op jit(solution)/shard_map/all_gather | solution.py:17
  39.6 9.8 %all_gather.20 = bf16[1280,384]{0,1:T(8,128)(2,1)S(1)} all-gather(bf16[1280,96]{0,1:T(8,128)(2,1)S(1)} %copy.23), channel_id=1, replica_groups=mesh['groups'=2,'vocab'=4,'rows'=4] {'rows'}, dimensions={1}, use_global_device_ids=true | all-gather | bytes 1228800 | tf_op jit(solution)/shard_map/all_gather | solution.py:17
  49.4 9.8 %all_gather.18 = bf16[1280,384]{0,1:T(8,128)(2,1)S(1)} all-gather(bf16[1280,96]{0,1:T(8,128)(2,1)S(1)} %copy.21), channel_id=1, replica_groups=mesh['groups'=2,'vocab'=4,'rows'=4] {'rows'}, dimensions={1}, use_global_device_ids=true | all-gather | bytes 1228800 | tf_op jit(solution)/shard_map/all_gather | solution.py:17
  59.3 2.8 gather_fusion
  62.1 0.6 convert_reduce_fusion
  62.7 1.3 ragged-dot-metadata
  64.0 3.8 sort.32
  67.8 2.1 all-gather.4.cloned.1.call-done
  69.9 2.5 fusion.8
  72.4 74.5 %all-gather.6.cloned.1.call-done = bf16[5120,384]{0,1:T(8,128)(2,1)} async-done(((bf16[1280,384]{0,1:T(8,128)(2,1)}), bf16[5120,384]{0,1:T(8,128)(2,1)}) %all-gather.6.cloned.1.call-update) | async-done | bytes 3932176 | tf_op jit(solution)/shard_map/all_gather | solution.py:35
  146.9 8.4 %ragged-dot-none = f32[384,128]{1,0:T(8,128)} custom-call(s32[1]{0:T(128)} %get-tuple-element.7, s32[4]{0:T(128)} %get-tuple-element.8, s32[5]{0:T(128)} %get-tuple-element.9, s32[5]{0:T(128)} %get-tuple-element.10, s32[1]{0:T(128)} %get-tuple-element.7, bf16[384,5120]{1,0:T(8,128)(2,1)} %bitcast.23, bf16[3,5120,128]{2,1,0:T(8,128)(2,1)} %param.8), custom_call_target="tpu_custom_call" | custom-call | flops 503316480 | bytes 8060940 | tf_op jit(solution)/shard_map/ragged_dot_general/ragged-dot-none
  155.2 2.0 gather_fusion.1
  157.3 0.1 copy.19
  157.4 0.1 reduce_max.18
  157.6 9.0 %all-reduce.2 = (f32[384]{0:T(512)S(1)}, f32[384]{0:T(512)S(1)}) all-reduce(f32[384]{0:T(512)S(1)} %get-tuple-element.33, f32[384]{0:T(512)S(1)} %reduce_max.18), channel_id=1, replica_groups=mesh['groups'=2,'vocab'=4,'rows'=4] {'vocab'}, use_global_device_ids=true, to_apply=%region_12.13 | all-reduce | flops 768 | bytes 6144 | tf_op jit(solution)/shard_map/pmax | solution.py:48
  166.6 0.2 exponential_reduce_fusion.1
  166.9 9.8 %all-reduce.1 = (f32[384]{0:T(512)S(1)}, f32[384]{0:T(512)S(1)}) all-reduce(f32[384]{0:T(512)S(1)} %exponential_reduce_fusion, f32[384]{0:T(512)S(1)} %exponential_reduce_fusion.1), channel_id=1, replica_groups=mesh['groups'=2,'vocab'=4,'rows'=4] {'vocab'}, use_global_device_ids=true, to_apply=%region_14.15 | all-reduce | flops 768 | bytes 6144 | tf_op jit(solution)/shard_map/psum | solution.py:51
  176.6 0.1 multiply_reduce_fusion
  176.7 9.0 %psum.38 = f32[384]{0:T(512)S(1)} all-reduce(f32[384]{0:T(512)S(1)} %get-tuple-element.17), channel_id=1, replica_groups=mesh['groups'=2,'vocab'=4,'rows'=4] {'vocab'}, use_global_device_ids=true, to_apply=%region_18.19 | all-reduce | flops 384 | bytes 3072 | tf_op jit(solution)/shard_map/psum | solution.py:62
  185.7 3.3 convolution_bitcast_fusion
  189.0 183.4 %all-reduce.4 = (f32[384]{0:T(512)}, bf16[3584,384]{0,1:T(8,128)(2,1)}) all-reduce(f32[384]{0:T(512)S(1)} %get-tuple-element.18, f32[3584,384]{0,1:T(8,128)} %convolution_bitcast_fusion), channel_id=1, replica_groups=mesh['groups'=2,'vocab'=4,'rows'=4] {'vocab'}, use_global_device_ids=true, to_apply=%region_16.17 | all-reduce | flops 1376640 | bytes 8260608 | tf_op jit(solution)/shard_map/psum | solution.py:62
  372.5 1.2 dynamic-slice_convert_fusion
  373.6 1.1 copy.20
  (22 shorter events, 0.3 us)
Async XLA Ops:
  7.2 62.7 %copy-start = (bf16[3584,128]{1,0:T(8,128)(2,1)S(1)}, bf16[3584,128]{1,0:T(8,128)(2,1)}, u32[]{:S(2)}) copy-start(bf16[3584,128]{1,0:T(8,128)(2,1)} %param.9) | copy-start | bytes 2752516
  7.2 7.7 %copy-start.2 = (s32[384]{0:T(512)S(1)}, s32[384]{0:T(512)}, u32[]{:S(2)}) copy-start(s32[384]{0:T(512)} %param.10) | copy-start | bytes 4612
  7.2 62.7 %all-gather.4.cloned.1.call-start = ((), (), s32[]{:S(2)}) async-start(), calls=%async_computation | async-start | bytes 3440640 | tf_op jit(solution)/shard_map/all_gather | solution.py:43
  7.9 138.9 %all-gather.6.cloned.1.call-start = ((), (), s32[]{:S(2)}) async-start(), calls=%async_computation.1 | async-start | bytes 4915200 | tf_op jit(solution)/shard_map/all_gather | solution.py:35
  185.7 3.3 copy-start.1
Sparse Core Ops, SparseCore 0:
  9.6 60.2 all-gather.3
  71.5 75.3 all-gather.5
where the time goes:
time: 382 us
  blocking collectives  252 us (66%)
  waiting for transfers between devices  77.3 us (20%)
  between operations  16.8 us (4%)
  other arithmetic  10.4 us (3%)
  local copies, waits for them, and re-layouts  9.87 us (3%)
  Pallas kernels  9.71 us (3%)
  matrix products  5.8 us (2%)
    psum x2, blocking collectives, local(): lax.psum((jnp.sum(p_teacher * (log_teacher - log_student), axis=1), jnp.s...  192 us
    all_gather x1, waiting for transfers between devices, local(): lax.all_gather(routed_sorted, 'vocab', axis=0, tiled=True)  74.5 us
    all_gather x4, blocking collectives, local(): gathered = lax.all_gather(row_block, 'rows', axis=1, tiled=True)  40.5 us
    psum x1, blocking collectives, local(): lax.psum((jnp.sum(jnp.exp(teacher_logits - t_peak[:, None]), axis=1), jnp...  9.75 us
    pmax x1, blocking collectives, local(): lax.pmax((jnp.max(teacher_logits, axis=1), jnp.max(student_logits, axis=1...  8.99 us
    another operation x1, Pallas kernels  8.38 us
  transfers between devices with their start and end apart: 2, of which 2 were waited for; matrix products, arithmetic and copies ran while one was open for 5% of the time, Pallas kernels for 0%

commit v1 on v0

--- a/solution.py
+++ b/solution.py
@@ -1,10 +1,330 @@
+import functools
+import math
+
 import jax
 import jax.numpy as jnp
 from jax import lax
+from jax.experimental import pallas as pl
+from jax.experimental.pallas import tpu as pltpu
 from jax.sharding import PartitionSpec as P
 
-
-def local(student_hidden, teacher_hidden, teacher_head, student_head, teacher_pick, owner):
+MESH = pl.DeviceIdType.MESH
+PART = jnp.float32
+VALUE_BOUND = 180.0 * 0.3125
+
+
+def part_scale(features):
+    return 2.0 ** -max(0, math.ceil(math.log2(features * VALUE_BOUND / 60000.0)))
+
+
+def window_kernel(
+    nz,
+    sub,
+    sh_ref,
+    th_ref,
+    thead_ref,
+    shead_ref,
+    pick_ref,
+    bmask_ref,
+    smask_ref,
+    kl_ref,
+    grad_ref,
+    wt,
+    ws,
+    sht,
+    tht,
+    own_t,
+    own_s,
+    send_t,
+    send_s,
+    recv_t,
+    recv_s,
+    tl_all,
+    dz_all,
+    kl_all,
+    pick_all,
+    local_sem,
+    zs_sem,
+    zr_sem,
+    ps_sem,
+    pr_sem,
+    ks_sem,
+    kr_sem,
+    ls_sem,
+    lr_sem,
+    rs_sem,
+    rr_sem,
+    ds_sem,
+    dr_sem,
+):
+    g = lax.axis_index("groups")
+    z = lax.axis_index("vocab")
+    r = lax.axis_index("rows")
+    x, c = r // 2, r % 2
+    rx = (1 - x) * 2 + c
+    rp = x * 2 + (1 - c)
+    ro = (1 - x) * 2 + (1 - c)
+    gy = 1 - g
+    dev_x, dev_y, dev_p = (g, z, rx), (gy, z, r), (g, z, rp)
+    row_peers = (rp, rx, ro)
+    own_p = (g * 4 + r, g * 4 + rx, gy * 4 + r, gy * 4 + rx)
+    mate_p = (g * 4 + rp, g * 4 + ro, gy * 4 + rp, gy * 4 + ro)
+    fwd_p = jnp.where(c == 0, own_p[1], own_p[2])
+    fwd_dev = (jnp.where(c == 0, gy, g), z, jnp.where(c == 0, r, rx))
+
+    ft, fs = th_ref.shape[0], sh_ref.shape[0]
+    bt, bs = ft // 8, fs // 8
+    vl = thead_ref.shape[2]
+
+    def t_at(piece, zz):
+        return wt.at[
+            :, pl.ds(pl.multiple_of(piece * bt, bt), bt), pl.ds(pl.multiple_of(zz * vl, vl), vl)
+        ]
+
+    def s_at(piece, zz):
+        return ws.at[
+            pl.ds(pl.multiple_of(piece * bs, bs), bs), pl.ds(pl.multiple_of(zz * vl, vl), vl)
+        ]
+
+    at = (s_at, t_at)
+
+    def remote(src, dst, ssem, rsem, dev):
+        return pltpu.make_async_remote_copy(
+            src_ref=src, dst_ref=dst, send_sem=ssem, recv_sem=rsem, device_id=dev, device_id_type=MESH
+        )
+
+    loc_t = pltpu.make_async_copy(
+        thead_ref.at[:, pl.ds(pl.multiple_of(z * ft, ft), ft), :],
+        wt.at[:, :, pl.ds(pl.multiple_of(z * vl, vl), vl)],
+        local_sem.at[0],
+    )
+    loc_s = pltpu.make_async_copy(
+        shead_ref.at[pl.ds(pl.multiple_of(z * fs, fs), fs), :],
+        ws.at[:, pl.ds(pl.multiple_of(z * vl, vl), vl)],
+        local_sem.at[1],
+    )
+    loc_s.start()
+    loc_t.start()
+
+    barrier = pltpu.get_barrier_semaphore()
+    peers = [(g, (z + d) % nz, r) for d in range(1, nz)]
+    peers += [(g, z, q) for q in row_peers] + [dev_y]
+    for dev in peers:
+        pl.semaphore_signal(barrier, inc=1, device_id=dev, device_id_type=MESH)
+    pl.semaphore_wait(barrier, len(peers))
+
+    sends = []
+
+    def go(copy):
+        copy.start()
+        sends.append(copy)
+
+    for a in range(2):
+        for d in range(1, nz):
+            zd = (z + d) % nz
+            if a == 0:
+                src = shead_ref.at[pl.ds(pl.multiple_of(zd * fs + own_p[0] * bs, bs), bs), :]
+            else:
+                src = thead_ref.at[:, pl.ds(pl.multiple_of(zd * ft + own_p[0] * bt, bt), bt), :]
+            go(
+                remote(
+                    src, at[a](own_p[0], z), zs_sem.at[a, d - 1], zr_sem.at[a, d - 1], (g, zd, r)
+                )
+            )
+    pick_all[r] = pick_ref[...]
+    for i, q in enumerate(row_peers):
+        go(remote(pick_all.at[r], pick_all.at[r], ks_sem.at[i], kr_sem.at[i], (g, z, q)))
+
+    sht[...] = sh_ref[...].T
+    tht[...] = th_ref[...].T
+
+    def plane(a, d, kind, piece, dev):
+        ref = at[a](piece, (z - d) % nz)
+        return remote(ref, ref, ps_sem.at[a, d - 1, kind], pr_sem.at[a, d - 1, kind], dev)
+
+    def stage1(a):
+        for d in range(1, nz):
+            zd = (z - d) % nz
+            dst = at[a](own_p[0], zd)
+            remote(dst, dst, zs_sem.at[a, d - 1], zr_sem.at[a, d - 1], (g, zd, r)).wait_recv()
+            go(plane(a, d, 0, own_p[0], dev_x))
+            go(plane(a, d, 1, own_p[0], dev_y))
+            go(plane(a, d, 3, own_p[0], dev_p))
+
+    def stage2(a):
+        for d in range(1, nz):
+            plane(a, d, 0, own_p[1], dev_x).wait_recv()
+            plane(a, d, 1, own_p[2], dev_y).wait_recv()
+            go(plane(a, d, 2, fwd_p, fwd_dev))
+            go(plane(a, d, 4, own_p[1], dev_p))
+            go(plane(a, d, 5, own_p[2], dev_p))
+
+    def stage3(a):
+        for d in range(1, nz):
+            plane(a, d, 2, own_p[3], dev_x).wait_recv()
+            go(plane(a, d, 6, own_p[3], dev_p))
+
+    def stage4(a):
+        for d in range(1, nz):
+            for i in range(4):
+                plane(a, d, 3 + i, mate_p[i], dev_p).wait_recv()
+
+    def exchange(a, own, send, recv, scale):
+        for d in range(1, nz):
+            zd = (z + d) % nz
+            send[zd] = (own[pl.ds(pl.multiple_of(zd * sub, sub), sub), :] * scale).astype(PART)
+            go(remote(send.at[zd], recv.at[z], ls_sem.at[a, d - 1], lr_sem.at[a, d - 1], (g, zd, r)))
+
+    def collect(a, own, recv, scale):
+        total = own[pl.ds(pl.multiple_of(z * sub, sub), sub), :]
+        for d in range(1, nz):
+            zd = (z - d) % nz
+            dst = recv.at[zd]
+            remote(dst, dst, ls_sem.at[a, d - 1], lr_sem.at[a, d - 1], (g, zd, r)).wait_recv()
+            total = total + recv[zd].astype(jnp.float32) * (1.0 / scale)
+        return total
+
+    stage1(0)
+    stage1(1)
+    stage2(0)
+    stage3(0)
+    stage2(1)
+    stage4(0)
+    loc_s.wait()
+    own_s[...] = jnp.dot(sht[...], ws[...], preferred_element_type=jnp.float32)
+    scale_s = part_scale(fs)
+    exchange(0, own_s, send_s, recv_s, scale_s)
+    stage3(1)
+
+    for i, q in enumerate(row_peers):
+        dst = pick_all.at[q]
+        remote(dst, dst, ks_sem.at[i], kr_sem.at[i], (g, z, q)).wait_recv()
+    picks = jnp.zeros_like(pick_ref)
+    for b in range(4):
+        picks = jnp.where(bmask_ref[b] > 0.5, pick_all[b], picks)
+    pick_t = jnp.broadcast_to(picks[0:1], (128, picks.shape[1])).T[:, 0:1]
+
+    stage4(1)
+    loc_t.wait()
+    logits = jnp.zeros(own_t.shape, jnp.float32)
+    for t in range(wt.shape[0]):
+        one = jnp.dot(tht[...], wt[t], preferred_element_type=jnp.float32)
+        logits = jnp.where(jnp.abs(pick_t - t) < 0.5, one, logits)
+    own_t[...] = logits
+    scale_t = part_scale(ft)
+    exchange(1, own_t, send_t, recv_t, scale_t)
+
+    student = collect(0, own_s, recv_s, scale_s)
+    s_shift = student - jnp.max(student, axis=1, keepdims=True)
+    log_s = s_shift - jnp.log(jnp.sum(jnp.exp(s_shift), axis=1, keepdims=True))
+    p_s = jnp.exp(log_s)
+
+    tl_all[r] = collect(1, own_t, recv_t, scale_t)
+    for i, q in enumerate(row_peers):
+        go(remote(tl_all.at[r], tl_all.at[r], rs_sem.at[i], rr_sem.at[i], (g, z, q)))
+    for i, q in enumerate(row_peers):
+        dst = tl_all.at[q]
+        remote(dst, dst, rs_sem.at[i], rr_sem.at[i], (g, z, q)).wait_recv()
+    teacher = tl_all[0]
+    for j in range(1, 4):
+        teacher = jnp.where(smask_ref[j, 0:1, :] > 0.5, tl_all[j], teacher)
+
+    t_shift = teacher - jnp.max(teacher, axis=1, keepdims=True)
+    log_t = t_shift - jnp.log(jnp.sum(jnp.exp(t_shift), axis=1, keepdims=True))
+    p_t = jnp.exp(log_t)
+    diff = log_s - log_t
+    fkl = -jnp.sum(p_t * diff, axis=1, keepdims=True)
+    rkl = jnp.sum(p_s * diff, axis=1, keepdims=True)
+    dz_all[z] = ((p_s - p_t) + p_s * (diff - rkl)).astype(jnp.bfloat16)
+    lane = lax.broadcasted_iota(jnp.int32, (sub, 128), 1)
+    both = jnp.where(lane == 0, fkl, rkl)
+    kl_all[z] = both.T[0:8, :]
+
+    for d in range(1, nz):
+        zd = (z + d) % nz
+        go(remote(dz_all.at[z], dz_all.at[z], ds_sem.at[0, d - 1], dr_sem.at[0, d - 1], (g, zd, r)))
+        go(remote(kl_all.at[z], kl_all.at[z], ds_sem.at[1, d - 1], dr_sem.at[1, d - 1], (g, zd, r)))
+    for d in range(1, nz):
+        zd = (z - d) % nz
+        for a, ref in ((0, dz_all), (1, kl_all)):
+            dst = ref.at[zd]
+            remote(dst, dst, ds_sem.at[a, d - 1], dr_sem.at[a, d - 1], (g, zd, r)).wait_recv()
+    for q in range(nz):
+        kl_ref[q] = kl_all[q]
+    dz = dz_all[...].reshape(nz * sub, dz_all.shape[2])
+    grad_ref[...] = lax.dot_general(
+        ws[...], dz, (((1,), (1,)), ((), ())), preferred_element_type=jnp.float32
+    ).astype(jnp.bfloat16)
+    for copy in sends:
+        copy.wait_send()
+
+
+def local_fast(student_hidden, teacher_hidden, teacher_head, student_head, teacher_pick, owner):
+    nz = lax.axis_size("vocab")
+    n_rows = lax.axis_size("rows")
+    fs, rows = student_hidden.shape
+    ft = teacher_hidden.shape[0]
+    teachers, _, vl = teacher_head.shape
+    sub = rows // owner.shape[0]
+    vocab = vl * nz
+    r = lax.axis_index("rows")
+    z = lax.axis_index("vocab")
+    ranks = jnp.arange(n_rows, dtype=jnp.int32)
+    pick = jnp.broadcast_to(teacher_pick.astype(jnp.float32)[None, :], (8, rows))
+    goes_to = jnp.repeat(lax.dynamic_index_in_dim(owner, r, 1, keepdims=False), sub)
+    bmask = jnp.broadcast_to(
+        (goes_to[None, None, :] == ranks[:, None, None]).astype(jnp.float32), (n_rows, 8, rows)
+    )
+    comes = (lax.dynamic_index_in_dim(owner, z, 0, keepdims=False) == r).astype(jnp.float32)
+    smask = jnp.broadcast_to(comes[:, None, None], (n_rows, 8, vocab))
+    vmem = pl.BlockSpec(memory_space=pltpu.VMEM)
+    hbm = pl.BlockSpec(memory_space=pl.ANY)
+    dma = pltpu.SemaphoreType.DMA
+    kl, grad = pl.pallas_call(
+        functools.partial(window_kernel, nz, sub),
+        out_shape=(
+            jax.ShapeDtypeStruct((nz, 8, sub), jnp.float32),
+            jax.ShapeDtypeStruct((fs, rows), jnp.bfloat16),
+        ),
+        in_specs=[vmem, vmem, hbm, hbm, vmem, vmem, vmem],
+        out_specs=(vmem, vmem),
+        scratch_shapes=[
+            pltpu.VMEM((teachers, ft, vocab), jnp.bfloat16),
+            pltpu.VMEM((fs, vocab), jnp.bfloat16),
+            pltpu.VMEM((rows, fs), jnp.bfloat16),
+            pltpu.VMEM((rows, ft), jnp.bfloat16),
+            pltpu.VMEM((rows, vocab), jnp.float32),
+            pltpu.VMEM((rows, vocab), jnp.float32),
+            pltpu.VMEM((nz, sub, vocab), PART),
+            pltpu.VMEM((nz, sub, vocab), PART),
+            pltpu.VMEM((nz, sub, vocab), PART),
+            pltpu.VMEM((nz, sub, vocab), PART),
+            pltpu.VMEM((n_rows, sub, vocab), jnp.float32),
+            pltpu.VMEM((nz, sub, vocab), jnp.bfloat16),
+            pltpu.VMEM((nz, 8, sub), jnp.float32),
+            pltpu.VMEM((n_rows, 8, rows), jnp.float32),
+            dma((2,)),
+            dma((2, nz - 1)),
+            dma((2, nz - 1)),
+            dma((2, nz - 1, 7)),
+            dma((2, nz - 1, 7)),
+            dma((3,)),
+            dma((3,)),
+            dma((2, nz - 1)),
+            dma((2, nz - 1)),
+            dma((3,)),
+            dma((3,)),
+            dma((2, nz - 1)),
+            dma((2, nz - 1)),
+        ],
+        compiler_params=pltpu.CompilerParams(
+            collective_id=0, has_side_effects=True, vmem_limit_bytes=40 * 1024 * 1024
+        ),
+    )(student_hidden, teacher_hidden, teacher_head, student_head, pick, bmask, smask)
+    return kl[:, 0, :].reshape(rows), kl[:, 1, :].reshape(rows), grad
+
+
+def local_any(student_hidden, teacher_hidden, teacher_head, student_head, teacher_pick, owner):
     rows_local = student_hidden.shape[1]
     round_count = owner.shape[0]
     sub_rows = rows_local // round_count
@@ -92,6 +412,13 @@
         P(("groups", "rows")),
         P("groups", None),
     )
+
+    def local(student_hidden, teacher_hidden, teacher_head, student_head, teacher_pick, owner):
+        args = (student_hidden, teacher_hidden, teacher_head, student_head, teacher_pick, owner)
+        sizes = (mesh.shape["groups"], mesh.shape["rows"], mesh.shape["vocab"])
+        fits = sizes == (2, 4, owner.shape[0]) and student_hidden.shape[0] % 128 == 0
+        return (local_fast if fits else local_any)(*args)
+
     return jax.shard_map(
         local,
         mesh=mesh,

time: 382 us -> 93.2 us (0.24)
  blocking collectives: 252 us -> 0 us
  waiting for transfers between devices: 77.3 us -> 0 us
  Pallas kernels: 9.71 us -> 81.4 us
  between operations: 16.8 us -> 0.66 us
  other arithmetic: 10.4 us -> 1.38 us
  matrix products: 5.8 us -> 0 us
    psum x3 -> x0, blocking collectives: 202 us -> none  [the longest x2 192 us: local(): lax.psum((jnp.sum(p_teacher * (log_teacher - log_student), axis=1), jnp.s...]
    pallas_call x0 -> x1, Pallas kernels: none -> 81.4 us  [local_fast(): pl.pallas_call(functools.partial(window_kernel, nz, sub), out_shape=(jax....]
    all_gather x2 -> x0, waiting for transfers between devices: 76.6 us -> none  [the longest x1 74.5 us: local(): lax.all_gather(routed_sorted, 'vocab', axis=0, tiled=True)]
    all_gather x4 -> x0, blocking collectives: 40.5 us -> none  [local(): gathered = lax.all_gather(row_block, 'rows', axis=1, tiled=True)]
    pmax x1 -> x0, blocking collectives: 8.99 us -> none  [local(): lax.pmax((jnp.max(teacher_logits, axis=1), jnp.max(student_logits, axis=1...]
    another operation x1 -> x0, Pallas kernels: 8.38 us -> none
    sort x2 -> x0, other arithmetic: 7.54 us -> none  [the longest x1 3.77 us: local(): row_order = jnp.argsort(teacher_pick, stable=True)]
    dot_general x2 -> x0, matrix products: 5.8 us -> none  [the longest x1 3.31 us: local(): lax.dot_general(head_rows, logit_grad, (((1,), (1,)), ((), ())), preferre...]
  transfers between devices with their start and end apart: 2 -> 0, of which waited for: 2 -> 0; matrix products, arithmetic and copies ran while one was open for 5% -> 0% of each run, Pallas kernels for 0% -> 0%
where the time goes in v1:
time: 93.2 us; the launch traced here: 92.3 us
  Pallas kernels  81.4 us (87%)
  local copies, waits for them, and re-layouts  8.89 us (10%)
  other arithmetic  1.38 us (1%)
    pallas_call x1, Pallas kernels, local_fast(): pl.pallas_call(functools.partial(window_kernel, nz, sub), out_shape=(jax....  81.4 us
    unnamed x9, local copies, waits for them, and re-layouts  6.44 us

profile of v1, /device:TPU:0, one launch (start us, length us, event | category | flops | bytes accessed | tf_op | source)
XLA Modules:
  0.0 92.3 jit_solution(16013992671095076374)
XLA Ops:
  0.6 0.7 fusion.1
  1.3 0.9 dynamic-slice_reduce_fusion
  2.2 0.1 broadcast_in_dim.9
  2.3 0.1 eq.31
  2.4 0.7 convert_element_type.21
  3.1 0.1 broadcast_in_dim.11.smask_ref
  3.1 0.0 copy-start
  3.1 2.1 %copy-done = bf16[3,5120,128]{2,1,0:T(8,128)(2,1)S(1)} copy-done((bf16[3,5120,128]{2,1,0:T(8,128)(2,1)S(1)}, bf16[3,5120,128]{2,1,0:T(8,128)(2,1)}, u32[]{:S(2)}) %copy-start) | copy-done | bytes 3932184
  5.2 0.0 copy-start.1
  5.3 1.2 %copy-done.1 = bf16[1280,384]{1,0:T(8,128)(2,1)S(1)} copy-done((bf16[1280,384]{1,0:T(8,128)(2,1)S(1)}, bf16[1280,384]{1,0:T(8,128)(2,1)}, u32[]{:S(2)}) %copy-start.1) | copy-done | bytes 983064
  6.5 0.0 copy-start.2
  6.5 1.2 %copy-done.2 = bf16[3584,128]{1,0:T(8,128)(2,1)S(1)} copy-done((bf16[3584,128]{1,0:T(8,128)(2,1)S(1)}, bf16[3584,128]{1,0:T(8,128)(2,1)}, u32[]{:S(2)}) %copy-start.2) | copy-done | bytes 917528
  7.6 0.0 copy-start.3
  7.6 1.1 %copy-done.3 = bf16[896,384]{1,0:T(8,128)(2,1)S(1)} copy-done((bf16[896,384]{1,0:T(8,128)(2,1)S(1)}, bf16[896,384]{1,0:T(8,128)(2,1)}, u32[]{:S(2)}) %copy-start.3) | copy-done | bytes 688152
  8.7 81.4 %shard_map.85 = (f32[4,8,96]{2,1,0:T(8,128)S(1)}, bf16[896,384]{1,0:T(8,128)(2,1)S(1)}) custom-call(bf16[896,384]{1,0:T(8,128)(2,1)S(1)} %copy-done.3, bf16[1280,384]{1,0:T(8,128)(2,1)S(1)} %copy-done.1, bf16[3,5120,128]{2,1,0:T(8,128)(2,1)S(1)} %copy-done, bf16[3584,128]{1,0:T(8,128)(2,1)S(1)} %copy-done.2, f32[8,384]{1,0:T(8,128)S(1)} %broadcast_in_dim.8.pick_ref, ...), custom_call_target="tpu_custom_call" | custom-call | tf_op jit(solution)/shard_map/pallas_call | solution.py:283
  90.1 0.7 reshape_squeeze.7
  90.8 0.7 reshape_squeeze.6
  91.4 0.8 copy.10
  (4 shorter events, 0.0 us)
Async XLA Ops:
  3.1 2.1 %copy-start = (bf16[3,5120,128]{2,1,0:T(8,128)(2,1)S(1)}, bf16[3,5120,128]{2,1,0:T(8,128)(2,1)}, u32[]{:S(2)}) copy-start(bf16[3,5120,128]{2,1,0:T(8,128)(2,1)} %thead_ref.1) | copy-start | bytes 11796484
  5.2 1.2 %copy-start.1 = (bf16[1280,384]{1,0:T(8,128)(2,1)S(1)}, bf16[1280,384]{1,0:T(8,128)(2,1)}, u32[]{:S(2)}) copy-start(bf16[1280,384]{1,0:T(8,128)(2,1)} %th_ref.1) | copy-start | bytes 2949124
  6.5 1.2 %copy-start.2 = (bf16[3584,128]{1,0:T(8,128)(2,1)S(1)}, bf16[3584,128]{1,0:T(8,128)(2,1)}, u32[]{:S(2)}) copy-start(bf16[3584,128]{1,0:T(8,128)(2,1)} %shead_ref.1) | copy-start | bytes 2752516
  7.6 1.1 %copy-start.3 = (bf16[896,384]{1,0:T(8,128)(2,1)S(1)}, bf16[896,384]{1,0:T(8,128)(2,1)}, u32[]{:S(2)}) copy-start(bf16[896,384]{1,0:T(8,128)(2,1)} %sh_ref.1) | copy-start | bytes 2064388

commit v2 on v1

--- a/solution.py
+++ b/solution.py
@@ -9,26 +9,40 @@
 from jax.sharding import PartitionSpec as P
 
 MESH = pl.DeviceIdType.MESH
-PART = jnp.float32
-VALUE_BOUND = 180.0 * 0.3125
-
-
-def part_scale(features):
-    return 2.0 ** -max(0, math.ceil(math.log2(features * VALUE_BOUND / 60000.0)))
+CODE_TOP = 32760.0
+CODE_UNIT = 4.0
+
+
+def code_range(x):
+    top = jnp.maximum(jnp.max(jnp.max(jnp.abs(x), axis=1, keepdims=True), axis=0, keepdims=True), 0.01)
+    top = top * (1.0 / CODE_UNIT)
+    return jnp.log(top + jnp.sqrt(top * top + 1.0))
+
+
+def encode(x, span):
+    y = jnp.abs(x) * (1.0 / CODE_UNIT)
+    y = jnp.log(y + jnp.sqrt(y * y + 1.0)) * (CODE_TOP / span) + 0.5
+    return jnp.where(x < 0, -y, y).astype(jnp.int32).astype(jnp.int16)
+
+
+def decode(code, span):
+    e = jnp.exp(code.astype(jnp.float32) * (span * (1.0 / CODE_TOP)))
+    return (e - 1.0 / e) * (0.5 * CODE_UNIT)
 
 
 def window_kernel(
     nz,
     sub,
-    sh_ref,
-    th_ref,
+    sh_hbm,
+    th_hbm,
     thead_ref,
     shead_ref,
     pick_ref,
-    bmask_ref,
-    smask_ref,
+    owner_ref,
     kl_ref,
     grad_ref,
+    sh_ref,
+    th_ref,
     wt,
     ws,
     sht,
@@ -39,7 +53,10 @@
     send_s,
     recv_t,
     recv_s,
+    meta_send,
+    meta_recv,
     tl_all,
+    tm_all,
     dz_all,
     kl_all,
     pick_all,
@@ -76,17 +93,16 @@
     bt, bs = ft // 8, fs // 8
     vl = thead_ref.shape[2]
 
-    def t_at(piece, zz):
-        return wt.at[
-            :, pl.ds(pl.multiple_of(piece * bt, bt), bt), pl.ds(pl.multiple_of(zz * vl, vl), vl)
-        ]
-
-    def s_at(piece, zz):
-        return ws.at[
-            pl.ds(pl.multiple_of(piece * bs, bs), bs), pl.ds(pl.multiple_of(zz * vl, vl), vl)
-        ]
-
-    at = (s_at, t_at)
+    def at(a, piece, zz):
+        cols = pl.ds(pl.multiple_of(zz * vl, vl), vl)
+        if a == 0:
+            return ws.at[pl.ds(pl.multiple_of(piece * bs, bs), bs), cols]
+        return wt.at[a - 1, pl.ds(pl.multiple_of(piece * bt, bt), bt), cols]
+
+    def head_at(a, zz):
+        if a == 0:
+            return shead_ref.at[pl.ds(pl.multiple_of(zz * fs + own_p[0] * bs, bs), bs), :]
+        return thead_ref.at[a - 1, pl.ds(pl.multiple_of(zz * ft + own_p[0] * bt, bt), bt), :]
 
     def remote(src, dst, ssem, rsem, dev):
         return pltpu.make_async_remote_copy(
@@ -103,8 +119,8 @@
         ws.at[:, pl.ds(pl.multiple_of(z * vl, vl), vl)],
         local_sem.at[1],
     )
-    loc_s.start()
-    loc_t.start()
+    loc_sh = pltpu.make_async_copy(sh_hbm, sh_ref, local_sem.at[2])
+    loc_th = pltpu.make_async_copy(th_hbm, th_ref, local_sem.at[3])
 
     barrier = pltpu.get_barrier_semaphore()
     peers = [(g, (z + d) % nz, r) for d in range(1, nz)]
@@ -119,33 +135,43 @@
         copy.start()
         sends.append(copy)
 
-    for a in range(2):
+    def stage0(a):
         for d in range(1, nz):
             zd = (z + d) % nz
-            if a == 0:
-                src = shead_ref.at[pl.ds(pl.multiple_of(zd * fs + own_p[0] * bs, bs), bs), :]
-            else:
-                src = thead_ref.at[:, pl.ds(pl.multiple_of(zd * ft + own_p[0] * bt, bt), bt), :]
             go(
                 remote(
-                    src, at[a](own_p[0], z), zs_sem.at[a, d - 1], zr_sem.at[a, d - 1], (g, zd, r)
+                    head_at(a, zd),
+                    at(a, own_p[0], z),
+                    zs_sem.at[a, d - 1],
+                    zr_sem.at[a, d - 1],
+                    (g, zd, r),
                 )
             )
-    pick_all[r] = pick_ref[...]
+
+    stage0(0)
+    stage0(1)
+    stage0(2)
+    loc_sh.start()
+    loc_th.start()
+    loc_s.start()
+    loc_t.start()
+    pick_all[r] = jnp.broadcast_to(pick_ref[...], pick_all.shape[1:])
     for i, q in enumerate(row_peers):
         go(remote(pick_all.at[r], pick_all.at[r], ks_sem.at[i], kr_sem.at[i], (g, z, q)))
 
+    loc_sh.wait()
     sht[...] = sh_ref[...].T
+    loc_th.wait()
     tht[...] = th_ref[...].T
 
     def plane(a, d, kind, piece, dev):
-        ref = at[a](piece, (z - d) % nz)
+        ref = at(a, piece, (z - d) % nz)
         return remote(ref, ref, ps_sem.at[a, d - 1, kind], pr_sem.at[a, d - 1, kind], dev)
 
     def stage1(a):
         for d in range(1, nz):
             zd = (z - d) % nz
-            dst = at[a](own_p[0], zd)
+            dst = at(a, own_p[0], zd)
             remote(dst, dst, zs_sem.at[a, d - 1], zr_sem.at[a, d - 1], (g, zd, r)).wait_recv()
             go(plane(a, d, 0, own_p[0], dev_x))
             go(plane(a, d, 1, own_p[0], dev_y))
@@ -169,65 +195,97 @@
             for i in range(4):
                 plane(a, d, 3 + i, mate_p[i], dev_p).wait_recv()
 
-    def exchange(a, own, send, recv, scale):
+    def exchange(a, own, send, recv):
         for d in range(1, nz):
             zd = (z + d) % nz
-            send[zd] = (own[pl.ds(pl.multiple_of(zd * sub, sub), sub), :] * scale).astype(PART)
-            go(remote(send.at[zd], recv.at[z], ls_sem.at[a, d - 1], lr_sem.at[a, d - 1], (g, zd, r)))
-
-    def collect(a, own, recv, scale):
+            part = own[pl.ds(pl.multiple_of(zd * sub, sub), sub), :]
+            span = code_range(part)
+            send[zd] = encode(part, span)
+            meta_send[a, zd] = jnp.broadcast_to(span, meta_send.shape[2:])
+            dev = (g, zd, r)
+            go(remote(send.at[zd], recv.at[z], ls_sem.at[a, d - 1], lr_sem.at[a, d - 1], dev))
+            go(
+                remote(
+                    meta_send.at[a, zd],
+                    meta_recv.at[a, z],
+                    ls_sem.at[2 + a, d - 1],
+                    lr_sem.at[2 + a, d - 1],
+                    dev,
+                )
+            )
+
+    def collect(a, own, recv):
         total = own[pl.ds(pl.multiple_of(z * sub, sub), sub), :]
         for d in range(1, nz):
             zd = (z - d) % nz
-            dst = recv.at[zd]
-            remote(dst, dst, ls_sem.at[a, d - 1], lr_sem.at[a, d - 1], (g, zd, r)).wait_recv()
-            total = total + recv[zd].astype(jnp.float32) * (1.0 / scale)
+            dst, meta = recv.at[zd], meta_recv.at[a, zd]
+            dev = (g, zd, r)
+            remote(dst, dst, ls_sem.at[a, d - 1], lr_sem.at[a, d - 1], dev).wait_recv()
+            remote(meta, meta, ls_sem.at[2 + a, d - 1], lr_sem.at[2 + a, d - 1], dev).wait_recv()
+            total = total + decode(recv[zd], meta_recv[a, zd][0:1, 0:1])
         return total
 
     stage1(0)
     stage1(1)
+    stage0(3)
     stage2(0)
+    stage2(1)
     stage3(0)
-    stage2(1)
+    stage1(2)
+    stage3(1)
+    stage2(2)
     stage4(0)
     loc_s.wait()
     own_s[...] = jnp.dot(sht[...], ws[...], preferred_element_type=jnp.float32)
-    scale_s = part_scale(fs)
-    exchange(0, own_s, send_s, recv_s, scale_s)
-    stage3(1)
+    stage1(3)
+    stage3(2)
+    stage2(3)
+    exchange(0, own_s, send_s, recv_s)
 
     for i, q in enumerate(row_peers):
         dst = pick_all.at[q]
         remote(dst, dst, ks_sem.at[i], kr_sem.at[i], (g, z, q)).wait_recv()
-    picks = jnp.zeros_like(pick_ref)
+    lanes = lax.broadcasted_iota(jnp.int32, pick_all.shape[1:], 1)
+    goes_to = jnp.zeros_like(lanes)
+    for k in range(nz):
+        goes_to = jnp.where(lanes >= k * sub, owner_ref[k, r], goes_to)
+    picks = jnp.zeros_like(lanes)
     for b in range(4):
-        picks = jnp.where(bmask_ref[b] > 0.5, pick_all[b], picks)
+        picks = jnp.where(goes_to == b, pick_all[b], picks)
+    picks = picks.astype(jnp.float32)
     pick_t = jnp.broadcast_to(picks[0:1], (128, picks.shape[1])).T[:, 0:1]
 
-    stage4(1)
     loc_t.wait()
-    logits = jnp.zeros(own_t.shape, jnp.float32)
     for t in range(wt.shape[0]):
+        if t == wt.shape[0] - 1:
+            stage3(t + 1)
+        stage4(t + 1)
         one = jnp.dot(tht[...], wt[t], preferred_element_type=jnp.float32)
-        logits = jnp.where(jnp.abs(pick_t - t) < 0.5, one, logits)
-    own_t[...] = logits
-    scale_t = part_scale(ft)
-    exchange(1, own_t, send_t, recv_t, scale_t)
-
-    student = collect(0, own_s, recv_s, scale_s)
+        own_t[...] = one if t == 0 else jnp.where(jnp.abs(pick_t - t) < 0.5, one, own_t[...])
+    exchange(1, own_t, send_t, recv_t)
+
+    student = collect(0, own_s, recv_s)
     s_shift = student - jnp.max(student, axis=1, keepdims=True)
     log_s = s_shift - jnp.log(jnp.sum(jnp.exp(s_shift), axis=1, keepdims=True))
     p_s = jnp.exp(log_s)
 
-    tl_all[r] = collect(1, own_t, recv_t, scale_t)
+    reduced = collect(1, own_t, recv_t)
+    span = code_range(reduced)
+    tl_all[r] = encode(reduced, span)
+    tm_all[r] = jnp.broadcast_to(span, tm_all.shape[1:])
     for i, q in enumerate(row_peers):
-        go(remote(tl_all.at[r], tl_all.at[r], rs_sem.at[i], rr_sem.at[i], (g, z, q)))
+        for a, ref in ((0, tl_all), (1, tm_all)):
+            go(remote(ref.at[r], ref.at[r], rs_sem.at[a, i], rr_sem.at[a, i], (g, z, q)))
     for i, q in enumerate(row_peers):
-        dst = tl_all.at[q]
-        remote(dst, dst, rs_sem.at[i], rr_sem.at[i], (g, z, q)).wait_recv()
-    teacher = tl_all[0]
+        for a, ref in ((0, tl_all), (1, tm_all)):
+            dst = ref.at[q]
+            remote(dst, dst, rs_sem.at[a, i], rr_sem.at[a, i], (g, z, q)).wait_recv()
+    wanted, span = tl_all[0].astype(jnp.int32), tm_all[0][0:1, 0:1]
     for j in range(1, 4):
-        teacher = jnp.where(smask_ref[j, 0:1, :] > 0.5, tl_all[j], teacher)
+        comes = owner_ref[z, j]
+        wanted = jnp.where(jnp.zeros_like(wanted) + comes == r, tl_all[j].astype(jnp.int32), wanted)
+        span = jnp.where(jnp.zeros((1, 1), jnp.int32) + comes == r, tm_all[j][0:1, 0:1], span)
+    teacher = decode(wanted, span)
 
     t_shift = teacher - jnp.max(teacher, axis=1, keepdims=True)
     log_t = t_shift - jnp.log(jnp.sum(jnp.exp(t_shift), axis=1, keepdims=True))
@@ -267,16 +325,6 @@
     teachers, _, vl = teacher_head.shape
     sub = rows // owner.shape[0]
     vocab = vl * nz
-    r = lax.axis_index("rows")
-    z = lax.axis_index("vocab")
-    ranks = jnp.arange(n_rows, dtype=jnp.int32)
-    pick = jnp.broadcast_to(teacher_pick.astype(jnp.float32)[None, :], (8, rows))
-    goes_to = jnp.repeat(lax.dynamic_index_in_dim(owner, r, 1, keepdims=False), sub)
-    bmask = jnp.broadcast_to(
-        (goes_to[None, None, :] == ranks[:, None, None]).astype(jnp.float32), (n_rows, 8, rows)
-    )
-    comes = (lax.dynamic_index_in_dim(owner, z, 0, keepdims=False) == r).astype(jnp.float32)
-    smask = jnp.broadcast_to(comes[:, None, None], (n_rows, 8, vocab))
     vmem = pl.BlockSpec(memory_space=pltpu.VMEM)
     hbm = pl.BlockSpec(memory_space=pl.ANY)
     dma = pltpu.SemaphoreType.DMA
@@ -286,41 +334,46 @@
             jax.ShapeDtypeStruct((nz, 8, sub), jnp.float32),
             jax.ShapeDtypeStruct((fs, rows), jnp.bfloat16),
         ),
-        in_specs=[vmem, vmem, hbm, hbm, vmem, vmem, vmem],
+        in_specs=[hbm, hbm, hbm, hbm, vmem, pl.BlockSpec(memory_space=pltpu.SMEM)],
         out_specs=(vmem, vmem),
         scratch_shapes=[
+            pltpu.VMEM((fs, rows), jnp.bfloat16),
+            pltpu.VMEM((ft, rows), jnp.bfloat16),
             pltpu.VMEM((teachers, ft, vocab), jnp.bfloat16),
             pltpu.VMEM((fs, vocab), jnp.bfloat16),
             pltpu.VMEM((rows, fs), jnp.bfloat16),
             pltpu.VMEM((rows, ft), jnp.bfloat16),
             pltpu.VMEM((rows, vocab), jnp.float32),
             pltpu.VMEM((rows, vocab), jnp.float32),
-            pltpu.VMEM((nz, sub, vocab), PART),
-            pltpu.VMEM((nz, sub, vocab), PART),
-            pltpu.VMEM((nz, sub, vocab), PART),
-            pltpu.VMEM((nz, sub, vocab), PART),
-            pltpu.VMEM((n_rows, sub, vocab), jnp.float32),
+            pltpu.VMEM((nz, sub, vocab), jnp.int16),
+            pltpu.VMEM((nz, sub, vocab), jnp.int16),
+            pltpu.VMEM((nz, sub, vocab), jnp.int16),
+            pltpu.VMEM((nz, sub, vocab), jnp.int16),
+            pltpu.VMEM((2, nz, 8, 128), jnp.float32),
+            pltpu.VMEM((2, nz, 8, 128), jnp.float32),
+            pltpu.VMEM((n_rows, sub, vocab), jnp.int16),
+            pltpu.VMEM((n_rows, 8, 128), jnp.float32),
             pltpu.VMEM((nz, sub, vocab), jnp.bfloat16),
             pltpu.VMEM((nz, 8, sub), jnp.float32),
-            pltpu.VMEM((n_rows, 8, rows), jnp.float32),
-            dma((2,)),
-            dma((2, nz - 1)),
-            dma((2, nz - 1)),
-            dma((2, nz - 1, 7)),
-            dma((2, nz - 1, 7)),
+            pltpu.VMEM((n_rows, 8, rows), jnp.int32),
+            dma((4,)),
+            dma((1 + teachers, nz - 1)),
+            dma((1 + teachers, nz - 1)),
+            dma((1 + teachers, nz - 1, 7)),
+            dma((1 + teachers, nz - 1, 7)),
             dma((3,)),
             dma((3,)),
-            dma((2, nz - 1)),
-            dma((2, nz - 1)),
-            dma((3,)),
-            dma((3,)),
+            dma((4, nz - 1)),
+            dma((4, nz - 1)),
+            dma((2, 3)),
+            dma((2, 3)),
             dma((2, nz - 1)),
             dma((2, nz - 1)),
         ],
         compiler_params=pltpu.CompilerParams(
-            collective_id=0, has_side_effects=True, vmem_limit_bytes=40 * 1024 * 1024
-        ),
-    )(student_hidden, teacher_hidden, teacher_head, student_head, pick, bmask, smask)
+            collective_id=0, has_side_effects=True, vmem_limit_bytes=58 * 1024 * 1024
+        ),
+    )(student_hidden, teacher_hidden, teacher_head, student_head, teacher_pick[None, :], owner)
     return kl[:, 0, :].reshape(rows), kl[:, 1, :].reshape(rows), grad
 
 
@@ -416,7 +469,7 @@
     def local(student_hidden, teacher_hidden, teacher_head, student_head, teacher_pick, owner):
         args = (student_hidden, teacher_hidden, teacher_head, student_head, teacher_pick, owner)
         sizes = (mesh.shape["groups"], mesh.shape["rows"], mesh.shape["vocab"])
-        fits = sizes == (2, 4, owner.shape[0]) and student_hidden.shape[0] % 128 == 0
+        fits = sizes == (2, 4, owner.shape[0]) and teacher_head.shape[0] == 3
         return (local_fast if fits else local_any)(*args)
 
     return jax.shard_map(

time: 93.2 us -> 70.9 us (0.76)
  Pallas kernels: 81.4 us -> 64.5 us
  local copies, waits for them, and re-layouts: 8.89 us -> 5.4 us
  other arithmetic: 1.38 us -> 0 us
    pallas_call x1, Pallas kernels: 81.4 us -> 64.5 us  [local_fast(): pl.pallas_call(functools.partial(window_kernel, nz, sub), out_shape=(jax....]
    unnamed x9 -> x1, local copies, waits for them, and re-layouts: 6.44 us -> 2.01 us
    convert_element_type x3 -> x0, other arithmetic: 1.38 us -> none  [the longest x1 0.69 us: local_fast(): (lax.dynamic_index_in_dim(owner, z, 0, keepdims=False) == r).astype(jnp.f...]
    broadcast_in_dim x4 -> x1, local copies, waits for them, and re-layouts: 0.15 us -> 1.25 us  [local_fast(): teacher_pick[None, :]]
where the time goes in v2:
time: 70.9 us; the launch traced here: 70.5 us
  Pallas kernels  64.5 us (91%)
  local copies, waits for them, and re-layouts  5.4 us (8%)
    pallas_call x1, Pallas kernels, local_fast(): pl.pallas_call(functools.partial(window_kernel, nz, sub), out_shape=(jax....  64.5 us
    unnamed x1, local copies, waits for them, and re-layouts  2.01 us

profile of v2, /device:TPU:0, one launch (start us, length us, event | category | flops | bytes accessed | tf_op | source)
XLA Modules:
  0.0 70.5 jit_solution(8551733889893129973)
XLA Ops:
  0.6 1.2 %broadcast_in_dim.3.pick_ref = s32[1,384]{1,0:T(1,128)} reshape(s32[384]{0:T(512)} %param.10) | data formatting | bytes 3072 | tf_op jit(solution)/shard_map/broadcast_in_dim | solution.py:376
  1.9 64.5 %shard_map.85 = (f32[4,8,96]{2,1,0:T(8,128)}, bf16[896,384]{1,0:T(8,128)(2,1)}) custom-call(bf16[896,384]{1,0:T(8,128)(2,1)} %sh_hbm.1, bf16[1280,384]{1,0:T(8,128)(2,1)} %th_hbm.1, bf16[3,5120,128]{2,1,0:T(8,128)(2,1)} %thead_ref.1, bf16[3584,128]{1,0:T(8,128)(2,1)} %shead_ref.1, s32[1,384]{1,0:T(1,128)} %broadcast_in_dim.3.pick_ref, s32[4,4]{1,0:T(4,128)} %owner_ref.1), custom_call_target="tpu_custom_call" | custom-call | tf_op jit(solution)/shard_map/pallas_call | solution.py:331
  66.3 0.8 %slice_reduce_fusion = (f32[4,96]{1,0:T(4,128)S(1)}, f32[4,96]{1,0:T(4,128)S(1)}) fusion(f32[4,8,96]{2,1,0:T(8,128)} %get-tuple-element.5), kind=kLoop, calls=%fused_computation | loop fusion | bytes 6144 | tf_op jit(solution)/shard_map/slice | solution.py:377
  67.1 0.7 reshape_squeeze.7
  67.8 0.7 reshape_squeeze.6
  68.5 2.0 %copy.10 = bf16[896,384]{1,0:T(8,128)(2,1)} copy(bf16[896,384]{1,0:T(8,128)(2,1)} %get-tuple-element.14) | data formatting | bytes 1376256
